TPU v7x, 32 devices: a whole 2x2x4 slice. The times are simulated.
32 devices in a mesh: patch: 8 (over z, y), mp: 4 (over x, core).
Axes of the slice: x: 2, y: 2, z: 4, core: 2. Of those that a mesh axis runs over, the one named last changes fastest.
Arguments:
- features: bfloat16 [4096, 1024], P('patch'), may hold values from -16 to 16
- gain_attn: float32 [1024], replicated, may hold values from 0.1 to 1.9
- w_qkv: bfloat16 [3, 1024, 1024], P(None, None, 'mp'), as said below
- w_out: bfloat16 [1024, 1024], P('mp'), may hold values from -0.1875 to 0.1875
- gain_mlp: float32 [1024], replicated, may hold values from 0.1 to 1.9
- w_up: bfloat16 [1024, 2048], P(None, 'mp'), may hold values from -0.1875 to 0.1875
- w_down: bfloat16 [2048, 1024], P('mp'), may hold values from -0.125 to 0.125
- neighbours: int32 [32, 8], replicated, may hold values from 0 to 31, as said below
Outputs:
- layer_out: bfloat16 [4096, 1024], P('patch', 'mp')
Inputs may be any that keep to these rules, and one draw needn't show every extreme that they name: `neighbours`: row p lists 8 different patches; the first is p itself. Patch q belongs to device q // 4 of the patch axis, and every listed patch belongs to a device whose index differs from that of p's device by at most 2 around the patch axis (the lining closes into a cycle). `w_qkv`: projection weights of mean zero.
All inputs are finite; a program needn't handle non-finite values.
Results may differ from a plain program's by a relative error of at most 0.012.
Values may be sent and summed in bfloat16 or wider, within the bound.
A program may use at most 64 MiB of HBM per device.

v0:
```python
import jax
import jax.numpy as jnp
from jax import lax
from jax.sharding import PartitionSpec as P

D = 1024
HD = 64
PN = 128
K_NB = 8
REACH = 2


def from_behind(array, axis, by):
    length = lax.axis_size(axis)
    return lax.ppermute(array, axis, [(i, (i + by) % length) for i in range(length)])


def normalize(rows, gain):
    rows32 = rows.astype(jnp.float32)
    mean_sq = jnp.mean(rows32 * rows32, axis=-1, keepdims=True)
    return (rows32 * lax.rsqrt(mean_sq + 1e-05) * gain).astype(jnp.bfloat16)


def per_device(features, gain_attn, w_qkv, w_out, gain_mlp, w_up, w_down, neighbours):
    row_count = features.shape[0]
    patches_here = row_count // PN
    heads_here = w_qkv.shape[2] // HD
    normed = normalize(features, gain_attn)
    queries = jnp.dot(normed, w_qkv[0], preferred_element_type=jnp.float32).astype(jnp.bfloat16)
    own_keys = (
        jnp.dot(normed, w_qkv[1], preferred_element_type=jnp.float32)
        .astype(jnp.bfloat16)
        .reshape(patches_here, PN, -1)
    )
    own_vals = (
        jnp.dot(normed, w_qkv[2], preferred_element_type=jnp.float32)
        .astype(jnp.bfloat16)
        .reshape(patches_here, PN, -1)
    )
    window = {0: (own_keys, own_vals)}
    for offset in range(-REACH, REACH + 1):
        if offset != 0:
            window[offset] = from_behind((own_keys, own_vals), "patch", -offset)
    keys_win = jnp.concatenate([window[offset][0] for offset in range(-REACH, REACH + 1)], axis=0)
    vals_win = jnp.concatenate([window[offset][1] for offset in range(-REACH, REACH + 1)], axis=0)
    device = lax.axis_index("patch")
    n_dev = lax.axis_size("patch")
    listed = lax.dynamic_slice_in_dim(neighbours, device * patches_here, patches_here, 0)
    owner_dev = listed // patches_here
    offset_dev = jnp.mod(owner_dev - device + n_dev // 2, n_dev) - n_dev // 2
    slot_index = (offset_dev + REACH) * patches_here + jnp.mod(listed, patches_here)
    keys_nb = keys_win[slot_index].reshape(patches_here, K_NB * PN, heads_here, HD)
    vals_nb = vals_win[slot_index].reshape(patches_here, K_NB * PN, heads_here, HD)
    query_blk = queries.reshape(patches_here, PN, heads_here, HD)
    scores = jnp.einsum(
        "pqhd,pkhd->phqk", query_blk, keys_nb, preferred_element_type=jnp.float32
    ) * (1.0 / HD**0.5)
    probs = jax.nn.softmax(scores, axis=-1).astype(jnp.bfloat16)
    mixed_rows = jnp.einsum("phqk,pkhd->pqhd", probs, vals_nb, preferred_element_type=jnp.float32)
    attended = mixed_rows.astype(jnp.bfloat16).reshape(row_count, heads_here * HD)
    partial_value = jnp.dot(attended, w_out, preferred_element_type=jnp.float32)
    col_share = lax.psum_scatter(
        partial_value.astype(jnp.bfloat16), "mp", scatter_dimension=1, tiled=True
    ).astype(jnp.float32)
    col_width = col_share.shape[1]
    col_begin = lax.axis_index("mp") * col_width
    residual_cols = (
        lax.dynamic_slice_in_dim(features, col_begin, col_width, 1).astype(jnp.float32) + col_share
    )
    gain_cols = lax.dynamic_slice_in_dim(gain_mlp, col_begin, col_width, 0)
    square_sum = lax.psum(jnp.sum(residual_cols * residual_cols, axis=1), "mp")
    inverse_rms = lax.rsqrt(square_sum / D + 1e-05)
    normed_cols = (residual_cols * inverse_rms[:, None] * gain_cols).astype(jnp.bfloat16)
    normed2 = lax.all_gather(normed_cols, "mp", axis=1, tiled=True)
    hidden = jax.nn.gelu(
        jnp.dot(normed2, w_up, preferred_element_type=jnp.float32), approximate=True
    ).astype(jnp.bfloat16)
    down_term = jnp.dot(hidden, w_down, preferred_element_type=jnp.float32)
    down_cols = lax.psum_scatter(
        down_term.astype(jnp.bfloat16), "mp", scatter_dimension=1, tiled=True
    ).astype(jnp.float32)
    return (residual_cols + down_cols).astype(jnp.bfloat16)


def solution(mesh):
    return jax.shard_map(
        per_device,
        mesh=mesh,
        in_specs=(
            P("patch", None),
            P(),
            P(None, None, "mp"),
            P("mp", None),
            P(),
            P(None, "mp"),
            P("mp", None),
            P(),
        ),
        out_specs=P("patch", "mp"),
        check_vma=False,
    )
```

profile of v0, /device:TPU:0, one launch (start us, length us, event | category | flops | bytes accessed | tf_op | source)
XLA Modules:
  0.0 168.8 jit_solution(17118276604014144791)
XLA Ops:
  6.6 1.7 fusion.9
  8.2 1.9 %convolution_convert_fusion.2 = bf16[512,256]{1,0:T(8,128)(2,1)S(1)} fusion(bf16[3,1024,256]{2,1,0:T(8,128)(2,1)} %param.10, bf16[512,1024]{1,0:T(8,128)(2,1)} %param.8, f32[1024]{0:T(1024)} %param.9, f32[512]{0:T(512)S(1)} %add_rsqrt_fusion.1), kind=kOutput, calls=%fused_computation.20 | convolution fusion | flops 270663680 | bytes 1841152 | tf_op jit(solution)/shard_map/dot_general | solution.py:31
  10.1 3.1 %collective-permute-start.4 = (bf16[4,128,256]{2,1,0:T(8,128)(2,1)S(1)}, bf16[4,128,256]{2,1,0:T(8,128)(2,1)}, u32[]{:S(2)}, u32[]{:S(2)}) collective-permute-start(bf16[4,128,256]{2,1,0:T(8,128)(2,1)S(1)} %bitcast.30), channel_id=1, source_target_pairs={{0,8},{4,12},{8,16},{12,20},{16,24},{20,28},{24,0},{28,4},{1,9},{5... | collective-permute-start | bytes 786440 | tf_op jit(solution)/shard_map/ppermute | solution.py:15
  13.2 1.5 collective-permute-start.5
  14.7 3.2 %collective-permute-start.6 = (bf16[4,128,256]{2,1,0:T(8,128)(2,1)S(1)}, bf16[4,128,256]{2,1,0:T(8,128)(2,1)S(1)}, u32[]{:S(2)}, u32[]{:S(2)}) collective-permute-start(bf16[4,128,256]{2,1,0:T(8,128)(2,1)S(1)} %bitcast.32), channel_id=1, source_target_pairs={{0,28},{4,0},{8,4},{12,8},{16,12},{20,16},{24,20},{28,24},{1,29},{... | collective-permute-start | bytes 786440 | tf_op jit(solution)/shard_map/ppermute | solution.py:15
  17.9 0.3 collective-permute-start.7
  18.2 0.5 convolution_convert_fusion.4
  18.7 1.8 %collective-permute-start = (bf16[4,128,256]{2,1,0:T(8,128)(2,1)S(1)}, bf16[4,128,256]{2,1,0:T(8,128)(2,1)}, u32[]{:S(2)}, u32[]{:S(2)}) collective-permute-start(bf16[4,128,256]{2,1,0:T(8,128)(2,1)S(1)} %bitcast.25), channel_id=1, source_target_pairs={{0,8},{4,12},{8,16},{12,20},{16,24},{20,28},{24,0},{28,4},{1,9},{5... | collective-permute-start | bytes 786440 | tf_op jit(solution)/shard_map/ppermute | solution.py:15
  20.5 0.5 convolution_convert_fusion.3
  21.0 0.1 compare_select_fusion
  21.1 0.1 copy.17
  21.2 0.1 reshape.39
  21.3 1.1 reshape.60
  22.3 0.1 collective-permute-done.4
  22.5 1.9 %collective-permute-start.1 = (bf16[4,128,256]{2,1,0:T(8,128)(2,1)S(1)}, bf16[4,128,256]{2,1,0:T(8,128)(2,1)}, u32[]{:S(2)}, u32[]{:S(2)}) collective-permute-start(bf16[4,128,256]{2,1,0:T(8,128)(2,1)S(1)} %bitcast.26), channel_id=1, source_target_pairs={{0,4},{4,8},{8,12},{12,16},{16,20},{20,24},{24,28},{28,0},{1,5},{5... | collective-permute-start | bytes 786440 | tf_op jit(solution)/shard_map/ppermute | solution.py:15
  24.4 1.7 constant_dynamic-update-slice_fusion.9
  26.0 3.3 %collective-permute-done.5 = bf16[4,128,256]{2,1,0:T(8,128)(2,1)} collective-permute-done((bf16[4,128,256]{2,1,0:T(8,128)(2,1)S(1)}, bf16[4,128,256]{2,1,0:T(8,128)(2,1)}, u32[]{:S(2)}, u32[]{:S(2)}) %collective-permute-start.5) | collective-permute-done | bytes 262176 | tf_op jit(solution)/shard_map/ppermute | solution.py:15
  29.3 1.7 constant_dynamic-update-slice_fusion.8
  31.0 0.7 constant_dynamic-update-slice_fusion.7
  31.7 11.0 %collective-permute-start.3 = (bf16[4,128,256]{2,1,0:T(8,128)(2,1)S(1)}, bf16[4,128,256]{2,1,0:T(8,128)(2,1)}, u32[]{:S(2)}, u32[]{:S(2)}) collective-permute-start(bf16[4,128,256]{2,1,0:T(8,128)(2,1)S(1)} %bitcast.28), channel_id=1, source_target_pairs={{0,24},{4,28},{8,0},{12,4},{16,8},{20,12},{24,16},{28,20},{1,25},{... | collective-permute-start | bytes 786440 | tf_op jit(solution)/shard_map/ppermute | solution.py:15
  42.7 0.7 constant_dynamic-update-slice_fusion.6
  43.4 0.7 constant_dynamic-update-slice_fusion.5
  44.1 2.0 %gather_fusion.1 = bf16[32,128,256]{2,1,0:T(8,128)(2,1)S(1)} fusion(bf16[20,128,256]{2,1,0:T(8,128)(2,1)} %constant_dynamic-update-slice_fusion.5, s32[1024]{0:T(1024)S(1)} %pad_clamp_fusion), kind=kCustom, calls=%fused_computation.1 | custom fusion | bytes 4194432 | tf_op jit(solution)/shard_map/gather | solution.py:52
  46.1 3.3 %reshape.61 = bf16[4,1024,4,64]{3,2,1,0:T(4,128)(2,1)} reshape(bf16[32,128,256]{2,1,0:T(8,128)(2,1)S(1)} %gather_fusion.1) | data formatting | bytes 4194304 | tf_op jit(solution)/shard_map/reshape | solution.py:52
  49.4 3.6 %fusion.4 = f32[4,4,128,1024]{3,2,1,0:T(8,128)S(1)} fusion(bf16[4,1024,4,64]{3,2,1,0:T(4,128)(2,1)} %reshape.61, bf16[4,128,4,64]{3,2,1,0:T(4,128)(2,1)} %reshape.60), kind=kOutput, calls=%fused_computation.7 | convolution fusion | flops 268435456 | bytes 10747904 | tf_op jit(solution)/shard_map/pqhd,pkhd->phqk/dot_general | solution.py:55
  53.0 2.2 %fusion.62 = f32[4,4,128]{2,1,0:T(4,128)S(1)} fusion(f32[4,4,128,1024]{3,2,1,0:T(8,128)S(1)} %fusion.4), kind=kOutput, calls=%fused_computation.87 | output fusion | flops 8389631 | bytes 8396800 | tf_op jit(solution)/shard_map/sub | solution.py:58
  55.2 1.0 copy-done.1
  56.2 1.7 %constant_dynamic-update-slice_fusion.4 = bf16[20,128,256]{2,1,0:T(8,128)(2,1)} fusion(bf16[4,128,256]{2,1,0:T(8,128)(2,1)} %collective-permute-done), kind=kLoop, calls=%fused_computation.54 | loop fusion | bytes 524288
  57.9 1.7 constant_dynamic-update-slice_fusion.3
  59.6 0.7 constant_dynamic-update-slice_fusion.2
  60.3 1.7 %constant_dynamic-update-slice_fusion.1 = bf16[20,128,256]{2,1,0:T(8,128)(2,1)} fusion(bf16[20,128,256]{2,1,0:T(8,128)(2,1)} %constant_dynamic-update-slice_fusion.2, bf16[4,128,256]{2,1,0:T(8,128)(2,1)} %collective-permute-done.2), kind=kLoop, calls=%fused_computation.51 | loop fusion | bytes 524288
  62.0 1.7 constant_dynamic-update-slice_fusion
  63.7 2.0 %gather_fusion = bf16[32,128,256]{2,1,0:T(8,128)(2,1)S(1)} fusion(bf16[20,128,256]{2,1,0:T(8,128)(2,1)} %constant_dynamic-update-slice_fusion, s32[1024]{0:T(1024)S(1)} %pad_clamp_fusion), kind=kCustom, calls=%fused_computation | custom fusion | bytes 4194432 | tf_op jit(solution)/shard_map/gather | solution.py:53
  65.7 3.3 %reshape.59 = bf16[4,1024,4,64]{3,2,1,0:T(4,128)(2,1)} reshape(bf16[32,128,256]{2,1,0:T(8,128)(2,1)S(1)} %gather_fusion) | data formatting | bytes 4194304 | tf_op jit(solution)/shard_map/reshape | solution.py:53
  69.0 12.1 %fusion.15 = bf16[4,128,4,64]{1,3,2,0:T(8,128)(2,1)S(1)} fusion(f32[4,4,128]{2,1,0:T(4,128)S(1)} %fusion.62, bf16[4,1024,4,64]{3,2,1,0:T(4,128)(2,1)} %reshape.59, f32[4,4,128,1024]{3,2,1,0:T(8,128)} %copy-done.1), kind=kOutput, calls=%fused_computation.24 | convolution fusion | flops 279055360 | bytes 10756096 | tf_op jit(solution)/shard_map/phqk,pkhd->pqhd/dot_general | solution.py:59
  81.1 0.2 copy.24
  81.3 1.4 convolution_convert_fusion
  82.8 0.0 all-gather.2.cloned.1.call-start
  82.8 0.8 dynamic_slice.11
  83.7 21.4 %reduce-scatter.3.cloned.1.call-done = bf16[512,256]{1,0:T(8,128)(2,1)} async-done(((bf16[512,1024]{1,0:T(8,128)(2,1)}), bf16[512,256]{1,0:T(8,128)(2,1)}) %reduce-scatter.3.cloned.1.call-update) | async-done | bytes 262160 | tf_op jit(solution)/shard_map/reduce_scatter | solution.py:62
  105.1 1.1 multiply_reduce_fusion.1
  106.2 5.8 %psum.7 = f32[512]{0:T(512)S(1)} all-reduce(f32[512]{0:T(512)S(1)} %multiply_reduce_fusion.1), channel_id=1, replica_groups=mesh['patch'=8,'mp'=4] {'mp'}, use_global_device_ids=true, to_apply=%region_5.6 | all-reduce | flops 512 | bytes 4096 | tf_op jit(solution)/shard_map/psum | solution.py:71
  112.0 1.8 %multiply_convert_fusion = bf16[512,256]{1,0:T(8,128)(2,1)} fusion(bf16[512,256]{1,0:T(8,128)(2,1)} %reduce-scatter.3.cloned.1.call-done, f32[256]{0:T(256)S(1)} %dynamic_slice.11, f32[512]{0:T(512)S(1)} %add_rsqrt_fusion, bf16[512,1024]{1,0:T(8,128)(2,1)S(1)} %copy-done.3, s32[]{:T(128)S(6)} %select_n.27), kind=kLoop, calls=%fused_computation.42 | loop fusion | flops 786432 | bytes 789508 | tf_op jit(solution)/shard_map/convert_element_type | solution.py:73
  113.8 0.0 reduce-scatter.5.cloned.1.call-start
  113.9 18.0 %all-gather.2.cloned.1.call-done = bf16[512,1024]{1,0:T(8,128)(2,1)} async-done(((bf16[512,256]{1,0:T(8,128)(2,1)}), bf16[512,1024]{1,0:T(8,128)(2,1)}) %all-gather.2.cloned.1.call-update) | async-done | bytes 1048592 | tf_op jit(solution)/shard_map/all_gather | solution.py:74
  131.9 3.6 %convolution_convert_fusion.1 = bf16[512,1024]{1,0:T(8,128)(2,1)} fusion(bf16[512,1024]{1,0:T(8,128)(2,1)S(1)} %copy-done, bf16[512,1024]{1,0:T(8,128)(2,1)} %all-gather.2.cloned.1.call-done, bf16[1024,512]{1,0:T(8,128)(2,1)S(1)} %copy-done.8), kind=kOutput, calls=%fused_computation.19 | convolution fusion | flops 1076625408 | bytes 4194304 | tf_op jit(solution)/shard_map/dot_general | solution.py:78
  135.5 25.0 %reduce-scatter.5.cloned.1.call-done = bf16[512,256]{1,0:T(8,128)(2,1)} async-done(((bf16[512,1024]{1,0:T(8,128)(2,1)}), bf16[512,256]{1,0:T(8,128)(2,1)}) %reduce-scatter.5.cloned.1.call-update) | async-done | bytes 262160 | tf_op jit(solution)/shard_map/reduce_scatter | solution.py:79
  160.5 1.8 %add_convert_fusion = bf16[512,256]{1,0:T(8,128)(2,1)} fusion(bf16[512,256]{1,0:T(8,128)(2,1)} %reduce-scatter.5.cloned.1.call-done, bf16[512,256]{1,0:T(8,128)(2,1)S(1)} %copy-done.4, bf16[512,1024]{1,0:T(8,128)(2,1)S(1)} %copy-done.3, s32[]{:T(128)S(6)} %select_n.27), kind=kLoop, calls=%fused_computation.37 | loop fusion | flops 786432 | bytes 1048580 | tf_op jit(solution)/shard_map/convert_element_type | solution.py:82
  (33 shorter events, 0.1 us)
Async XLA Ops:
  6.5 125.3 %copy-start = (bf16[512,1024]{1,0:T(8,128)(2,1)S(1)}, bf16[512,1024]{1,0:T(8,128)(2,1)}, u32[]{:S(2)}) copy-start(bf16[512,1024]{1,0:T(8,128)(2,1)} %param.14) | copy-start | bytes 3145732
  6.5 11.7 %copy-start.2 = (bf16[512,1024]{1,0:T(8,128)(2,1)S(1)}, bf16[512,1024]{1,0:T(8,128)(2,1)}, u32[]{:S(2)}) copy-start(bf16[512,1024]{1,0:T(8,128)(2,1)} %param.8) | copy-start | bytes 3145732
  6.5 11.7 %copy-start.9 = (f32[1024]{0:T(1024)S(1)}, f32[1024]{0:T(1024)}, u32[]{:S(2)}) copy-start(f32[1024]{0:T(1024)} %param.9) | copy-start | bytes 12292
  6.5 98.6 %reduce-scatter.3.cloned.1.call-start = ((), (), s32[]{:S(2)}) async-start(), calls=%async_computation.2 | async-start | bytes 1310720 | tf_op jit(solution)/shard_map/reduce_scatter | solution.py:62
  6.5 11.7 %copy-start.7 = (bf16[3,1024,256]{2,1,0:T(8,128)(2,1)S(1)}, bf16[3,1024,256]{2,1,0:T(8,128)(2,1)}, u32[]{:S(2)}) copy-start(bf16[3,1024,256]{2,1,0:T(8,128)(2,1)} %param.10) | copy-start | bytes 4718596
  10.1 12.4 %collective-permute-start.4 = (bf16[4,128,256]{2,1,0:T(8,128)(2,1)S(1)}, bf16[4,128,256]{2,1,0:T(8,128)(2,1)}, u32[]{:S(2)}, u32[]{:S(2)}) collective-permute-start(bf16[4,128,256]{2,1,0:T(8,128)(2,1)S(1)} %bitcast.30), channel_id=1, source_target_pairs={{0,8},{4,12},{8,16},{12,20},{16,24},{20,28},{24,0},{28,4},{1,9},{5... | collective-permute-start | bytes 786440 | tf_op jit(solution)/shard_map/ppermute | solution.py:15
  13.2 16.1 %collective-permute-start.5 = (bf16[4,128,256]{2,1,0:T(8,128)(2,1)S(1)}, bf16[4,128,256]{2,1,0:T(8,128)(2,1)}, u32[]{:S(2)}, u32[]{:S(2)}) collective-permute-start(bf16[4,128,256]{2,1,0:T(8,128)(2,1)S(1)} %bitcast.31), channel_id=1, source_target_pairs={{0,4},{4,8},{8,12},{12,16},{16,20},{20,24},{24,28},{28,0},{1,5},{5... | collective-permute-start | bytes 786440 | tf_op jit(solution)/shard_map/ppermute | solution.py:15
  14.7 17.0 %collective-permute-start.6 = (bf16[4,128,256]{2,1,0:T(8,128)(2,1)S(1)}, bf16[4,128,256]{2,1,0:T(8,128)(2,1)S(1)}, u32[]{:S(2)}, u32[]{:S(2)}) collective-permute-start(bf16[4,128,256]{2,1,0:T(8,128)(2,1)S(1)} %bitcast.32), channel_id=1, source_target_pairs={{0,28},{4,0},{8,4},{12,8},{16,12},{20,16},{24,20},{28,24},{1,29},{... | collective-permute-start | bytes 786440 | tf_op jit(solution)/shard_map/ppermute | solution.py:15
  17.9 25.5 %collective-permute-start.7 = (bf16[4,128,256]{2,1,0:T(8,128)(2,1)S(1)}, bf16[4,128,256]{2,1,0:T(8,128)(2,1)S(1)}, u32[]{:S(2)}, u32[]{:S(2)}) collective-permute-start(bf16[4,128,256]{2,1,0:T(8,128)(2,1)S(1)} %bitcast.33), channel_id=1, source_target_pairs={{0,24},{4,28},{8,0},{12,4},{16,8},{20,12},{24,16},{28,20},{1,25},{... | collective-permute-start | bytes 786440 | tf_op jit(solution)/shard_map/ppermute | solution.py:15
  18.7 2.3 %copy-start.6 = (s32[32,8]{0,1:T(8,128)S(1)}, s32[32,8]{0,1:T(8,128)}, u32[]{:S(2)}) copy-start(s32[32,8]{0,1:T(8,128)} %param.15) | copy-start | bytes 3076
  18.7 37.5 %collective-permute-start = (bf16[4,128,256]{2,1,0:T(8,128)(2,1)S(1)}, bf16[4,128,256]{2,1,0:T(8,128)(2,1)}, u32[]{:S(2)}, u32[]{:S(2)}) collective-permute-start(bf16[4,128,256]{2,1,0:T(8,128)(2,1)S(1)} %bitcast.25), channel_id=1, source_target_pairs={{0,8},{4,12},{8,16},{12,20},{16,24},{20,28},{24,0},{28,4},{1,9},{5... | collective-permute-start | bytes 786440 | tf_op jit(solution)/shard_map/ppermute | solution.py:15
  22.5 35.4 %collective-permute-start.1 = (bf16[4,128,256]{2,1,0:T(8,128)(2,1)S(1)}, bf16[4,128,256]{2,1,0:T(8,128)(2,1)}, u32[]{:S(2)}, u32[]{:S(2)}) collective-permute-start(bf16[4,128,256]{2,1,0:T(8,128)(2,1)S(1)} %bitcast.26), channel_id=1, source_target_pairs={{0,4},{4,8},{8,12},{12,16},{16,20},{20,24},{24,28},{28,0},{1,5},{5... | collective-permute-start | bytes 786440 | tf_op jit(solution)/shard_map/ppermute | solution.py:15
  29.3 31.0 %collective-permute-start.2 = (bf16[4,128,256]{2,1,0:T(8,128)(2,1)S(1)}, bf16[4,128,256]{2,1,0:T(8,128)(2,1)}, u32[]{:S(2)}, u32[]{:S(2)}) collective-permute-start(bf16[4,128,256]{2,1,0:T(8,128)(2,1)S(1)} %bitcast.27), channel_id=1, source_target_pairs={{0,28},{4,0},{8,4},{12,8},{16,12},{20,16},{24,20},{28,24},{1,29},{... | collective-permute-start | bytes 786440 | tf_op jit(solution)/shard_map/ppermute | solution.py:15
  31.7 30.4 %collective-permute-start.3 = (bf16[4,128,256]{2,1,0:T(8,128)(2,1)S(1)}, bf16[4,128,256]{2,1,0:T(8,128)(2,1)}, u32[]{:S(2)}, u32[]{:S(2)}) collective-permute-start(bf16[4,128,256]{2,1,0:T(8,128)(2,1)S(1)} %bitcast.28), channel_id=1, source_target_pairs={{0,24},{4,28},{8,0},{12,4},{16,8},{20,12},{24,16},{28,20},{1,25},{... | collective-permute-start | bytes 786440 | tf_op jit(solution)/shard_map/ppermute | solution.py:15
  53.0 3.2 %copy-start.1 = (f32[4,4,128,1024]{3,2,1,0:T(8,128)}, f32[4,4,128,1024]{3,2,1,0:T(8,128)S(1)}, u32[]{:S(2)}) copy-start(f32[4,4,128,1024]{3,2,1,0:T(8,128)S(1)} %fusion.4) | copy-start | bytes 25165828
  69.0 12.4 %copy-start.5 = (bf16[256,1024]{1,0:T(8,128)(2,1)S(1)}, bf16[256,1024]{1,0:T(8,128)(2,1)}, u32[]{:S(2)}) copy-start(bf16[256,1024]{1,0:T(8,128)(2,1)} %param.11) | copy-start | bytes 1572868
  81.1 24.0 %copy-start.3 = (bf16[512,1024]{1,0:T(8,128)(2,1)S(1)}, bf16[512,1024]{1,0:T(8,128)(2,1)}, u32[]{:S(2)}) copy-start(bf16[512,1024]{1,0:T(8,128)(2,1)} %param.8) | copy-start | bytes 3145732
  82.8 49.1 %copy-start.8 = (bf16[1024,512]{1,0:T(8,128)(2,1)S(1)}, bf16[1024,512]{1,0:T(8,128)(2,1)}, u32[]{:S(2)}) copy-start(bf16[1024,512]{1,0:T(8,128)(2,1)} %param.13) | copy-start | bytes 3145732
  82.8 49.1 %all-gather.2.cloned.1.call-start = ((), (), s32[]{:S(2)}) async-start(), calls=%async_computation.3 | async-start | bytes 1310720 | tf_op jit(solution)/shard_map/all_gather | solution.py:74
  113.8 46.7 %copy-start.4 = (bf16[512,256]{1,0:T(8,128)(2,1)S(1)}, bf16[512,256]{1,0:T(8,128)(2,1)}, u32[]{:S(2)}) copy-start(bf16[512,256]{1,0:T(8,128)(2,1)} %reduce-scatter.3.cloned.1.call-done) | copy-start | bytes 786436
  113.8 46.7 %reduce-scatter.5.cloned.1.call-start = ((), (), s32[]{:S(2)}) async-start(), calls=%async_computation.4 | async-start | bytes 1310720 | tf_op jit(solution)/shard_map/reduce_scatter | solution.py:79
Sparse Core Ops, SparseCore 0:
  82.9 22.1 reduce-scatter.2
  113.9 17.9 all-gather.1
  135.6 24.8 reduce-scatter.4
where the time goes:
time: 169 us
  waiting for transfers between devices  68 us (40%)
  local copies, waits for them, and re-layouts  26.8 us (16%)
  matrix products  23.6 us (14%)
  starting transfers between devices  22.8 us (13%)
  between operations  13.3 us (8%)
  other arithmetic  8.61 us (5%)
  blocking collectives  5.76 us (3%)
    reduce_scatter x1, waiting for transfers between devices, per_device(): lax.psum_scatter(down_term.astype(jnp.bfloat16), 'mp', scatter_dimension=...  25 us
    ppermute x8, starting transfers between devices, from_behind(): lax.ppermute(array, axis, [(i, (i + by) % length) for i in range(length)])  22.8 us
    reduce_scatter x1, waiting for transfers between devices, per_device(): lax.psum_scatter(partial_value.astype(jnp.bfloat16), 'mp', scatter_dimens...  21.4 us
    all_gather x1, waiting for transfers between devices, per_device(): normed2 = lax.all_gather(normed_cols, 'mp', axis=1, tiled=True)  18 us
    dot_general x1, matrix products, per_device(): jnp.einsum('phqk,pkhd->pqhd', probs, vals_nb, preferred_element_type=jnp....  12.1 us
    unnamed x28, local copies, waits for them, and re-layouts  11.6 us
    psum x1, blocking collectives, per_device(): square_sum = lax.psum(jnp.sum(residual_cols * residual_cols, axis=1), 'mp')  5.76 us
    dot_general x1, matrix products, per_device(): jnp.einsum('pqhd,pkhd->phqk', query_blk, keys_nb, preferred_element_type=...  3.62 us
  transfers between devices with their start and end apart: 11, of which 5 were waited for; matrix products, arithmetic and copies ran while one was open for 15% of the time, Pallas kernels for 0%

commit v1 on v0

v1 whole, which is shorter than its diff:
```python
import functools

import jax
import jax.numpy as jnp
from jax import lax
from jax.experimental import pallas as pl
from jax.experimental.pallas import tpu as pltpu
from jax.sharding import PartitionSpec as P

HD = 64
PN = 128
K_NB = 8
REACH = 2
N_MP = 4
MESH = pl.DeviceIdType.MESH
F32 = jnp.float32
BF16 = jnp.bfloat16


def rms(rows, gain):
    mean_sq = jnp.mean(rows * rows, axis=-1, keepdims=True)
    return (rows * lax.rsqrt(mean_sq + 1e-05) * gain).astype(BF16)


def kernel(
    n, per, nb, feats, gain_attn, w_qkv, w_out_in, gain_mlp, w_up_in, w_down_in, out,
    win, normed, stacked, near, w_out, w_up, w_down, att, res, down, half, part, last,
    local_sem, halo_s, halo_r, w_s, w_r, att_s, att_r, rs1_s, rs1_r, rs2_s, rs2_r,
):
    p = lax.axis_index("patch")
    m = lax.axis_index("mp")
    odd = lax.rem(p, 2)
    twin = p + 1 - 2 * odd
    ahead = lax.rem(p + REACH, n)
    behind = lax.rem(p + n - REACH, n)
    lo = lax.rem(m, 2)
    hi = m // 2
    m1 = m + 1 - 2 * lo
    m2 = m + 2 - 4 * hi
    width = att.shape[-1]
    own = REACH * per

    local = [
        pltpu.make_async_copy(w_out_in, w_out.at[m], local_sem.at[0]),
        pltpu.make_async_copy(w_up_in, w_up, local_sem.at[1]),
        pltpu.make_async_copy(w_down_in, w_down, local_sem.at[2]),
    ]
    for copy in local:
        copy.start()

    barrier = pltpu.get_barrier_semaphore()
    for peer in (ahead, behind, twin):
        pl.semaphore_signal(barrier, inc=1, device_id={"patch": peer}, device_id_type=MESH)
    for peer in (m1, m2):
        pl.semaphore_signal(barrier, inc=1, device_id={"mp": peer}, device_id_type=MESH)
    pl.semaphore_wait(barrier, 5)

    def remote(src, dst, send, recv, where):
        return pltpu.make_async_remote_copy(
            src_ref=src, dst_ref=dst, send_sem=send, recv_sem=recv, device_id=where, device_id_type=MESH
        )

    def halo(kind, c):
        if kind == 0:
            src, dst, where = own + c, c, ahead
        elif kind == 1:
            src, dst, where = own + c, 4 * per + c, behind
        elif kind == 2:
            src, dst, where = own + c, (1 + 2 * odd) * per + c, twin
        else:
            src, dst, where = (4 - 4 * odd) * per + c, (3 - 2 * odd) * per + c, twin
        return remote(win.at[src], win.at[dst], halo_s.at[kind, c], halo_r.at[kind, c], {"patch": where})

    def halo_arrived(kind, c):
        dst = win.at[own + c]
        remote(dst, dst, halo_s.at[3, c], halo_r.at[kind, c], {"patch": twin}).wait_recv()

    def weight(kind):
        block = w_out.at[m if kind < 2 else m2]
        return remote(block, block, w_s.at[kind], w_r.at[kind], {"mp": m2 if kind == 0 else m1})

    def gather(kind, c):
        block = att.at[c, m if kind < 2 else m2]
        return remote(block, block, att_s.at[kind, c], att_r.at[kind, c], {"mp": m2 if kind == 0 else m1})

    def first_sum(c):
        return remote(down.at[c, 1 - lo], half.at[c], rs1_s.at[c], rs1_r.at[c], {"mp": m1})

    def second_sum(c):
        return remote(part.at[c], last.at[c], rs2_s.at[c], rs2_r.at[c], {"mp": m2})

    def project(c, carry):
        rows = pl.ds(pl.multiple_of(c * PN, PN), PN)
        here = rms(feats[rows, :].astype(F32), gain_attn[...])
        normed[rows, :] = here
        win[own + c, :, :width] = jnp.dot(here, w_qkv[1], preferred_element_type=F32).astype(BF16)
        win[own + c, :, width:] = jnp.dot(here, w_qkv[2], preferred_element_type=F32).astype(BF16)
        for kind in (0, 1, 2):
            halo(kind, c).start()
        return carry

    lax.fori_loop(0, per, project, 0)

    local[0].wait()
    weight(0).start()
    weight(1).start()

    heads = width // HD
    head_of = lax.broadcasted_iota(jnp.int32, (PN, width), 1) // HD

    def query(c, carry):
        rows = pl.ds(pl.multiple_of(c * PN, PN), PN)
        q = jnp.dot(normed[rows, :], w_qkv[0], preferred_element_type=F32).astype(BF16).astype(F32) * (1.0 / HD**0.5)
        for h in range(heads):
            stacked[c, h * PN : (h + 1) * PN, :] = jnp.where(head_of == h, q, 0.0).astype(BF16)
        return carry

    lax.fori_loop(0, per, query, 0)

    def forward(c, carry):
        halo_arrived(1 - odd, c)
        halo(3, c).start()
        return carry

    lax.fori_loop(0, per, forward, 0)
    weight(0).wait_recv()
    weight(2).start()

    def arrived(c, carry):
        halo_arrived(odd, c)
        halo_arrived(2, c)
        halo_arrived(3, c)
        return carry

    lax.fori_loop(0, per, arrived, 0)

    def attend(c, carry):
        for j in range(K_NB):
            listed = nb[p * per + c, j]
            offset = lax.rem(listed // per - p + n + n // 2, n) - n // 2
            slot = jnp.clip((offset + REACH) * per + lax.rem(listed, per), 0, (2 * REACH + 1) * per - 1)
            near[j * PN : (j + 1) * PN, :] = win[slot]
        mixed = jnp.zeros((PN, width), F32)
        for h in range(0, heads, 2):
            scores = lax.dot_general(
                stacked[c, h * PN : (h + 2) * PN, :], near[:, :width], (((1,), (1,)), ((), ())),
                preferred_element_type=F32,
            )
            top = jnp.max(scores, axis=-1, keepdims=True)
            e = jnp.exp(scores - top)
            total = jnp.sum(e, axis=-1, keepdims=True)
            o = jnp.dot(e.astype(BF16), near[:, width:], preferred_element_type=F32) / total
            mixed = jnp.where(head_of == h, o[:PN], mixed)
            mixed = jnp.where(head_of == h + 1, o[PN:], mixed)
        att[c, m] = mixed.astype(BF16)
        gather(0, c).start()
        gather(1, c).start()

        @pl.when(c > 0)
        def _():
            gather(0, c - 1).wait_recv()
            gather(2, c - 1).start()

        return carry

    lax.fori_loop(0, per, attend, 0)
    weight(1).wait_recv()
    weight(2).wait_recv()
    local[1].wait()
    local[2].wait()

    def add_up(c):
        first_sum(c).wait_recv()
        part[c] = (down[c, lo, 1 - hi].astype(F32) + half[c, 1 - hi].astype(F32)).astype(BF16)
        second_sum(c).start()

    def mlp(c, carry):
        @pl.when(c == 0)
        def _():
            gather(0, per - 1).wait_recv()
            gather(2, per - 1).start()

        gather(1, c).wait_recv()
        gather(2, c).wait_recv()
        rows = pl.ds(pl.multiple_of(c * PN, PN), PN)
        residual = feats[rows, :].astype(F32)
        for g in range(N_MP):
            residual = residual + jnp.dot(att[c, g], w_out[g], preferred_element_type=F32)
        for g in range(N_MP):
            res[c, g] = residual[:, g * width : (g + 1) * width]
        normed2 = rms(residual, gain_mlp[...])
        hidden = jax.nn.gelu(jnp.dot(normed2, w_up[...], preferred_element_type=F32), approximate=True).astype(BF16)
        for g in range(N_MP):
            down[c, g % 2, g // 2] = jnp.dot(
                hidden, w_down[:, g * width : (g + 1) * width], preferred_element_type=F32
            ).astype(BF16)
        first_sum(c).start()

        @pl.when(c > 0)
        def _():
            add_up(c - 1)

        return carry

    lax.fori_loop(0, per, mlp, 0)
    add_up(per - 1)

    def finish(c, carry):
        second_sum(c).wait_recv()
        rows = pl.ds(pl.multiple_of(c * PN, PN), PN)
        total = down[c, lo, hi].astype(F32) + half[c, hi].astype(F32) + last[c].astype(F32)
        out[rows, :] = (res[c, m] + total).astype(BF16)
        return carry

    lax.fori_loop(0, per, finish, 0)

    def sent(c, carry):
        for kind in range(4):
            halo(kind, c).wait_send()
        for kind in range(3):
            gather(kind, c).wait_send()
        first_sum(c).wait_send()
        second_sum(c).wait_send()
        return carry

    lax.fori_loop(0, per, sent, 0)
    for kind in range(3):
        weight(kind).wait_send()


def per_device(n, features, gain_attn, w_qkv, w_out, gain_mlp, w_up, w_down, neighbours):
    rows, d = features.shape
    per = rows // PN
    width = w_qkv.shape[2]
    heads = width // HD
    units = w_up.shape[1]
    vmem = pl.BlockSpec(memory_space=pltpu.VMEM)
    anywhere = pl.BlockSpec(memory_space=pl.ANY)
    dma = pltpu.SemaphoreType.DMA
    return pl.pallas_call(
        functools.partial(kernel, n, per),
        out_shape=jax.ShapeDtypeStruct((rows, d // N_MP), BF16),
        in_specs=[
            pl.BlockSpec(memory_space=pltpu.SMEM), vmem, vmem, vmem, anywhere, vmem, anywhere, anywhere,
        ],
        out_specs=vmem,
        scratch_shapes=[
            pltpu.VMEM(((2 * REACH + 1) * per, PN, 2 * width), BF16),
            pltpu.VMEM((rows, d), BF16),
            pltpu.VMEM((per, heads * PN, width), BF16),
            pltpu.VMEM((K_NB * PN, 2 * width), BF16),
            pltpu.VMEM((N_MP, width, d), BF16),
            pltpu.VMEM((d, units), BF16),
            pltpu.VMEM((units, d), BF16),
            pltpu.VMEM((per, N_MP, PN, width), BF16),
            pltpu.VMEM((per, N_MP, PN, width), F32),
            pltpu.VMEM((per, 2, 2, PN, width), BF16),
            pltpu.VMEM((per, 2, PN, width), BF16),
            pltpu.VMEM((per, PN, width), BF16),
            pltpu.VMEM((per, PN, width), BF16),
            dma((3,)), dma((4, per)), dma((4, per)), dma((3,)), dma((3,)), dma((3, per)), dma((3, per)),
            dma((per,)), dma((per,)), dma((per,)), dma((per,)),
        ],
        compiler_params=pltpu.CompilerParams(
            collective_id=0, has_side_effects=True, vmem_limit_bytes=48 * 1024 * 1024
        ),
    )(neighbours, features, gain_attn.reshape(1, d), w_qkv, w_out, gain_mlp.reshape(1, d), w_up, w_down)


def solution(mesh):
    return jax.shard_map(
        functools.partial(per_device, mesh.shape["patch"]),
        mesh=mesh,
        in_specs=(
            P("patch", None),
            P(),
            P(None, None, "mp"),
            P("mp", None),
            P(),
            P(None, "mp"),
            P("mp", None),
            P(),
        ),
        out_specs=P("patch", "mp"),
        check_vma=False,
    )
```

time: 169 us -> 64.3 us (0.38)
  waiting for transfers between devices: 68 us -> 0 us
  Pallas kernels: 0 us -> 54.9 us
  matrix products: 23.6 us -> 0 us
  starting transfers between devices: 22.8 us -> 0 us
  local copies, waits for them, and re-layouts: 26.8 us -> 8.96 us
  between operations: 13.3 us -> 0.02 us
  other arithmetic: 8.61 us -> 0 us
  blocking collectives: 5.76 us -> 0 us
    pallas_call x0 -> x1, Pallas kernels: none -> 54.9 us  [per_device(): pl.pallas_call(functools.partial(kernel, n, per), out_shape=jax.ShapeDtyp...]
    reduce_scatter x2 -> x0, waiting for transfers between devices: 46.4 us -> none  [the longest x1 25 us: per_device(): lax.psum_scatter(down_term.astype(jnp.bfloat16), 'mp', scatter_dimension=...]
    dot_general x7 -> x0, matrix products: 23.6 us -> none  [the longest x1 12.1 us: per_device(): jnp.einsum('phqk,pkhd->pqhd', probs, vals_nb, preferred_element_type=jnp....]
    ppermute x8 -> x0, starting transfers between devices: 22.8 us -> none  [from_behind(): lax.ppermute(array, axis, [(i, (i + by) % length) for i in range(length)])]
    all_gather x1 -> x0, waiting for transfers between devices: 18 us -> none  [per_device(): normed2 = lax.all_gather(normed_cols, 'mp', axis=1, tiled=True)]
    reshape x3 -> x0, local copies, waits for them, and re-layouts: 7.59 us -> none  [the longest x1 3.28 us: per_device(): vals_win[slot_index].reshape(patches_here, K_NB * PN, heads_here, HD)]
    psum x1 -> x0, blocking collectives: 5.76 us -> none  [per_device(): square_sum = lax.psum(jnp.sum(residual_cols * residual_cols, axis=1), 'mp')]
    gather x2 -> x0, local copies, waits for them, and re-layouts: 3.99 us -> none  [the longest x1 2 us: per_device(): keys_win[slot_index].reshape(patches_here, K_NB * PN, heads_here, HD)]
  transfers between devices with their start and end apart: 11 -> 0, of which waited for: 5 -> 0; matrix products, arithmetic and copies ran while one was open for 15% -> 0% of each run, Pallas kernels for 0% -> 0%
where the time goes in v1:
time: 64.3 us; the launch traced here: 63.9 us
  Pallas kernels  54.9 us (85%)
  local copies, waits for them, and re-layouts  8.96 us (14%)
    pallas_call x1, Pallas kernels, per_device(): pl.pallas_call(functools.partial(kernel, n, per), out_shape=jax.ShapeDtyp...  54.9 us
    unnamed x16, local copies, waits for them, and re-layouts  8.96 us

profile of v1, /device:TPU:0, one launch (start us, length us, event | category | flops | bytes accessed | tf_op | source)
XLA Modules:
  0.0 63.9 jit_solution(8299186108271240697)
XLA Ops:
  0.0 0.8 %copy.9.nb = s32[32,8]{1,0:T(8,128)S(1)} copy(s32[32,8]{0,1:T(8,128)} %param.15) | data formatting | bytes 2048 | tf_op args[7]
  0.8 0.0 copy-start
  0.8 1.4 %copy-done = bf16[3,1024,256]{2,1,0:T(8,128)(2,1)S(1)} copy-done((bf16[3,1024,256]{2,1,0:T(8,128)(2,1)S(1)}, bf16[3,1024,256]{2,1,0:T(8,128)(2,1)}, u32[]{:S(2)}) %copy-start) | copy-done | bytes 1572888
  2.2 0.0 copy-start.1
  2.2 1.2 %copy-done.1 = bf16[512,1024]{1,0:T(8,128)(2,1)S(1)} copy-done((bf16[512,1024]{1,0:T(8,128)(2,1)S(1)}, bf16[512,1024]{1,0:T(8,128)(2,1)}, u32[]{:S(2)}) %copy-start.1) | copy-done | bytes 1048600
  3.4 0.0 copy-start.2
  3.4 1.2 %copy-done.2 = bf16[1024,512]{1,0:T(8,128)(2,1)S(1)} copy-done((bf16[1024,512]{1,0:T(8,128)(2,1)S(1)}, bf16[1024,512]{1,0:T(8,128)(2,1)}, u32[]{:S(2)}) %copy-start.2) | copy-done | bytes 1048600
  4.6 0.0 copy-start.3
  4.6 1.2 %copy-done.3 = bf16[512,1024]{1,0:T(8,128)(2,1)S(1)} copy-done((bf16[512,1024]{1,0:T(8,128)(2,1)S(1)}, bf16[512,1024]{1,0:T(8,128)(2,1)}, u32[]{:S(2)}) %copy-start.3) | copy-done | bytes 1048600
  5.8 0.0 copy-start.4
  5.8 1.0 %copy-done.4 = bf16[256,1024]{1,0:T(8,128)(2,1)S(1)} copy-done((bf16[256,1024]{1,0:T(8,128)(2,1)S(1)}, bf16[256,1024]{1,0:T(8,128)(2,1)}, u32[]{:S(2)}) %copy-start.4) | copy-done | bytes 524312
  6.9 0.0 copy-start.5
  6.9 0.7 %copy-done.5 = f32[1024]{0:T(1024)S(1)} copy-done((f32[1024]{0:T(1024)S(1)}, f32[1024]{0:T(1024)}, u32[]{:S(2)}) %copy-start.5) | copy-done | bytes 4120
  7.6 0.0 copy-start.6
  7.6 0.7 %copy-done.6 = f32[1024]{0:T(1024)S(1)} copy-done((f32[1024]{0:T(1024)S(1)}, f32[1024]{0:T(1024)}, u32[]{:S(2)}) %copy-start.6) | copy-done | bytes 4120
  8.3 54.9 %shard_map.82 = bf16[512,256]{1,0:T(8,128)(2,1)S(1)} custom-call(s32[32,8]{1,0:T(8,128)S(1)} %copy.9.nb, bf16[512,1024]{1,0:T(8,128)(2,1)S(1)} %copy-done.1, f32[1,1024]{1,0:T(1,128)S(1)} %bitcast.2, bf16[3,1024,256]{2,1,0:T(8,128)(2,1)S(1)} %copy-done, bf16[256,1024]{1,0:T(8,128)(2,1)S(1)} %copy-done.4, f32[1,1024]{1,0:T(1,128)S(1)} %bitcast.3, ...), custom_call_target="tpu_custom_call" | custom-call | tf_op jit(solution)/shard_map/pallas_call | solution.py:240
  63.2 0.7 %copy.11 = bf16[512,256]{1,0:T(8,128)(2,1)} copy(bf16[512,256]{1,0:T(8,128)(2,1)S(1)} %shard_map.82) | data formatting | bytes 524288
Async XLA Ops:
  0.8 1.4 %copy-start = (bf16[3,1024,256]{2,1,0:T(8,128)(2,1)S(1)}, bf16[3,1024,256]{2,1,0:T(8,128)(2,1)}, u32[]{:S(2)}) copy-start(bf16[3,1024,256]{2,1,0:T(8,128)(2,1)} %w_qkv.1) | copy-start | bytes 4718596
  2.2 1.2 %copy-start.1 = (bf16[512,1024]{1,0:T(8,128)(2,1)S(1)}, bf16[512,1024]{1,0:T(8,128)(2,1)}, u32[]{:S(2)}) copy-start(bf16[512,1024]{1,0:T(8,128)(2,1)} %feats.1) | copy-start | bytes 3145732
  3.4 1.2 %copy-start.2 = (bf16[1024,512]{1,0:T(8,128)(2,1)S(1)}, bf16[1024,512]{1,0:T(8,128)(2,1)}, u32[]{:S(2)}) copy-start(bf16[1024,512]{1,0:T(8,128)(2,1)} %w_up_in.1) | copy-start | bytes 3145732
  4.6 1.2 %copy-start.3 = (bf16[512,1024]{1,0:T(8,128)(2,1)S(1)}, bf16[512,1024]{1,0:T(8,128)(2,1)}, u32[]{:S(2)}) copy-start(bf16[512,1024]{1,0:T(8,128)(2,1)} %w_down_in.1) | copy-start | bytes 3145732
  5.8 1.0 %copy-start.4 = (bf16[256,1024]{1,0:T(8,128)(2,1)S(1)}, bf16[256,1024]{1,0:T(8,128)(2,1)}, u32[]{:S(2)}) copy-start(bf16[256,1024]{1,0:T(8,128)(2,1)} %w_out_in.1) | copy-start | bytes 1572868
  6.9 0.7 %copy-start.5 = (f32[1024]{0:T(1024)S(1)}, f32[1024]{0:T(1024)}, u32[]{:S(2)}) copy-start(f32[1024]{0:T(1024)} %param.9) | copy-start | bytes 12292
  7.6 0.7 %copy-start.6 = (f32[1024]{0:T(1024)S(1)}, f32[1024]{0:T(1024)}, u32[]{:S(2)}) copy-start(f32[1024]{0:T(1024)} %param.12) | copy-start | bytes 12292

commit v2 on v1

--- a/solution.py
+++ b/solution.py
@@ -23,8 +23,8 @@
 
 
 def kernel(
-    n, per, nb, feats, gain_attn, w_qkv, w_out_in, gain_mlp, w_up_in, w_down_in, out,
-    win, normed, stacked, near, w_out, w_up, w_down, att, res, down, half, part, last,
+    n, per, nb, feats_in, gain_attn_in, w_qkv_in, w_out_in, gain_mlp_in, w_up_in, w_down_in, out,
+    feats, gains, w_qkv, win, normed, stacked, near, w_out, w_up, w_down, att, res, down, half, part, last,
     local_sem, halo_s, halo_r, w_s, w_r, att_s, att_r, rs1_s, rs1_r, rs2_s, rs2_r,
 ):
     p = lax.axis_index("patch")
@@ -40,13 +40,23 @@
     width = att.shape[-1]
     own = REACH * per
 
-    local = [
-        pltpu.make_async_copy(w_out_in, w_out.at[m], local_sem.at[0]),
-        pltpu.make_async_copy(w_up_in, w_up, local_sem.at[1]),
-        pltpu.make_async_copy(w_down_in, w_down, local_sem.at[2]),
-    ]
-    for copy in local:
-        copy.start()
+    def take(which):
+        if which < per:
+            rows = pl.ds(which * PN, PN)
+            src, dst = feats_in.at[rows], feats.at[rows]
+        elif which < per + 3:
+            src, dst = w_qkv_in.at[which - per], w_qkv.at[which - per]
+        else:
+            src, dst = (
+                (gain_attn_in, gains.at[0]), (w_out_in, w_out.at[m]), (gain_mlp_in, gains.at[1]),
+                (w_up_in, w_up), (w_down_in, w_down),
+            )[which - per - 3]
+        return pltpu.make_async_copy(src, dst, local_sem.at[which])
+
+    take_q, take_k, take_v = per, per + 1, per + 2
+    take_gain, take_out, take_gain2, take_up, take_down = range(per + 3, per + 8)
+    for which in (take_gain, 0, take_k, take_v, *range(1, per), take_out, take_q, take_gain2, take_up, take_down):
+        take(which).start()
 
     barrier = pltpu.get_barrier_semaphore()
     for peer in (ahead, behind, twin):
@@ -89,19 +99,22 @@
     def second_sum(c):
         return remote(part.at[c], last.at[c], rs2_s.at[c], rs2_r.at[c], {"mp": m2})
 
-    def project(c, carry):
-        rows = pl.ds(pl.multiple_of(c * PN, PN), PN)
-        here = rms(feats[rows, :].astype(F32), gain_attn[...])
-        normed[rows, :] = here
+    for c in range(per):
+        take(c).wait()
+        if c == 0:
+            take(take_gain).wait()
+        here = rms(feats[c * PN : (c + 1) * PN, :].astype(F32), gains[0])
+        normed[c * PN : (c + 1) * PN, :] = here
+        if c == 0:
+            take(take_k).wait()
         win[own + c, :, :width] = jnp.dot(here, w_qkv[1], preferred_element_type=F32).astype(BF16)
+        if c == 0:
+            take(take_v).wait()
         win[own + c, :, width:] = jnp.dot(here, w_qkv[2], preferred_element_type=F32).astype(BF16)
         for kind in (0, 1, 2):
             halo(kind, c).start()
-        return carry
-
-    lax.fori_loop(0, per, project, 0)
-
-    local[0].wait()
+
+    take(take_out).wait()
     weight(0).start()
     weight(1).start()
 
@@ -115,6 +128,7 @@
             stacked[c, h * PN : (h + 1) * PN, :] = jnp.where(head_of == h, q, 0.0).astype(BF16)
         return carry
 
+    take(take_q).wait()
     lax.fori_loop(0, per, query, 0)
 
     def forward(c, carry):
@@ -136,7 +150,7 @@
 
     def attend(c, carry):
         for j in range(K_NB):
-            listed = nb[p * per + c, j]
+            listed = nb[j, p * per + c]
             offset = lax.rem(listed // per - p + n + n // 2, n) - n // 2
             slot = jnp.clip((offset + REACH) * per + lax.rem(listed, per), 0, (2 * REACH + 1) * per - 1)
             near[j * PN : (j + 1) * PN, :] = win[slot]
@@ -166,8 +180,8 @@
     lax.fori_loop(0, per, attend, 0)
     weight(1).wait_recv()
     weight(2).wait_recv()
-    local[1].wait()
-    local[2].wait()
+    for which in (take_gain2, take_up, take_down):
+        take(which).wait()
 
     def add_up(c):
         first_sum(c).wait_recv()
@@ -188,7 +202,7 @@
             residual = residual + jnp.dot(att[c, g], w_out[g], preferred_element_type=F32)
         for g in range(N_MP):
             res[c, g] = residual[:, g * width : (g + 1) * width]
-        normed2 = rms(residual, gain_mlp[...])
+        normed2 = rms(residual, gains[1])
         hidden = jax.nn.gelu(jnp.dot(normed2, w_up[...], preferred_element_type=F32), approximate=True).astype(BF16)
         for g in range(N_MP):
             down[c, g % 2, g // 2] = jnp.dot(
@@ -240,11 +254,12 @@
     return pl.pallas_call(
         functools.partial(kernel, n, per),
         out_shape=jax.ShapeDtypeStruct((rows, d // N_MP), BF16),
-        in_specs=[
-            pl.BlockSpec(memory_space=pltpu.SMEM), vmem, vmem, vmem, anywhere, vmem, anywhere, anywhere,
-        ],
+        in_specs=[pl.BlockSpec(memory_space=pltpu.SMEM)] + [anywhere] * 7,
         out_specs=vmem,
         scratch_shapes=[
+            pltpu.VMEM((rows, d), BF16),
+            pltpu.VMEM((2, 1, d), F32),
+            pltpu.VMEM((3, d, width), BF16),
             pltpu.VMEM(((2 * REACH + 1) * per, PN, 2 * width), BF16),
             pltpu.VMEM((rows, d), BF16),
             pltpu.VMEM((per, heads * PN, width), BF16),
@@ -258,13 +273,13 @@
             pltpu.VMEM((per, 2, PN, width), BF16),
             pltpu.VMEM((per, PN, width), BF16),
             pltpu.VMEM((per, PN, width), BF16),
-            dma((3,)), dma((4, per)), dma((4, per)), dma((3,)), dma((3,)), dma((3, per)), dma((3, per)),
+            dma((per + 8,)), dma((4, per)), dma((4, per)), dma((3,)), dma((3,)), dma((3, per)), dma((3, per)),
             dma((per,)), dma((per,)), dma((per,)), dma((per,)),
         ],
         compiler_params=pltpu.CompilerParams(
-            collective_id=0, has_side_effects=True, vmem_limit_bytes=48 * 1024 * 1024
+            collective_id=0, has_side_effects=True, vmem_limit_bytes=62 * 1024 * 1024
         ),
-    )(neighbours, features, gain_attn.reshape(1, d), w_qkv, w_out, gain_mlp.reshape(1, d), w_up, w_down)
+    )(neighbours.T, features, gain_attn.reshape(1, d), w_qkv, w_out, gain_mlp.reshape(1, d), w_up, w_down)
 
 
 def solution(mesh):

time: 64.3 us -> 58.3 us (0.907)
  local copies, waits for them, and re-layouts: 8.96 us -> 1.67 us
  Pallas kernels: 54.9 us -> 56.5 us
    unnamed x16 -> x1, local copies, waits for them, and re-layouts: 8.96 us -> 1.67 us
    pallas_call x1, Pallas kernels: 54.9 us -> 56.5 us  [per_device(): pl.pallas_call(functools.partial(kernel, n, per), out_shape=jax.ShapeDtyp...]
where the time goes in v2:
time: 58.3 us; the launch traced here: 58.1 us
  Pallas kernels  56.5 us (97%)
  local copies, waits for them, and re-layouts  1.67 us (3%)
    pallas_call x1, Pallas kernels, per_device(): pl.pallas_call(functools.partial(kernel, n, per), out_shape=jax.ShapeDtyp...  56.5 us
    unnamed x1, local copies, waits for them, and re-layouts  1.67 us

profile of v2, /device:TPU:0, one launch (start us, length us, event | category | flops | bytes accessed | tf_op | source)
XLA Modules:
  0.0 58.1 jit_solution(10050381599895054782)
XLA Ops:
  0.0 56.5 %shard_map.82 = bf16[512,256]{1,0:T(8,128)(2,1)} custom-call(s32[8,32]{1,0:T(8,128)} %bitcast.3, bf16[512,1024]{1,0:T(8,128)(2,1)} %feats_in.1, f32[1,1024]{1,0:T(1,128)} %bitcast.4, bf16[3,1024,256]{2,1,0:T(8,128)(2,1)} %w_qkv_in.1, bf16[256,1024]{1,0:T(8,128)(2,1)} %w_out_in.1, f32[1,1024]{1,0:T(1,128)} %bitcast.5, bf16[1024,512]{1,0:T(8,128)(2,1)} %w_up_in.1, ...), custom_call_target="tpu_custom_call" | custom-call | tf_op jit(solution)/shard_map/pallas_call | solution.py:254
  56.5 1.7 %copy.10 = bf16[512,256]{1,0:T(8,128)(2,1)} copy(bf16[512,256]{1,0:T(8,128)(2,1)} %shard_map.82) | data formatting | bytes 524288

commit v3 on v2

--- a/solution.py
+++ b/solution.py
@@ -70,16 +70,20 @@
             src_ref=src, dst_ref=dst, send_sem=send, recv_sem=recv, device_id=where, device_id_type=MESH
         )
 
+    relayed, direct = 1 - odd, odd
+
+    def reach(kind, c):
+        where = lax.rem(p + n + REACH - 2 * REACH * kind, n)
+        return remote(
+            win.at[own + c], win.at[4 * per * kind + c], halo_s.at[kind, c], halo_r.at[kind, c], {"patch": where}
+        )
+
     def halo(kind, c):
-        if kind == 0:
-            src, dst, where = own + c, c, ahead
-        elif kind == 1:
-            src, dst, where = own + c, 4 * per + c, behind
-        elif kind == 2:
-            src, dst, where = own + c, (1 + 2 * odd) * per + c, twin
+        if kind == 2:
+            src, dst = own + c, (1 + 2 * odd) * per + c
         else:
-            src, dst, where = (4 - 4 * odd) * per + c, (3 - 2 * odd) * per + c, twin
-        return remote(win.at[src], win.at[dst], halo_s.at[kind, c], halo_r.at[kind, c], {"patch": where})
+            src, dst = (4 - 4 * odd) * per + c, (3 - 2 * odd) * per + c
+        return remote(win.at[src], win.at[dst], halo_s.at[kind, c], halo_r.at[kind, c], {"patch": twin})
 
     def halo_arrived(kind, c):
         dst = win.at[own + c]
@@ -111,8 +115,8 @@
         if c == 0:
             take(take_v).wait()
         win[own + c, :, width:] = jnp.dot(here, w_qkv[2], preferred_element_type=F32).astype(BF16)
-        for kind in (0, 1, 2):
-            halo(kind, c).start()
+        reach(relayed, c).start()
+        halo(2, c).start()
 
     take(take_out).wait()
     weight(0).start()
@@ -131,22 +135,26 @@
     take(take_q).wait()
     lax.fori_loop(0, per, query, 0)
 
-    def forward(c, carry):
-        halo_arrived(1 - odd, c)
+    for c in range(per):
+        halo_arrived(relayed, c)
         halo(3, c).start()
-        return carry
-
-    lax.fori_loop(0, per, forward, 0)
+        if c == max(per - 2, 0):
+            for d in range(per):
+                reach(direct, d).start()
     weight(0).wait_recv()
     weight(2).start()
 
     def arrived(c, carry):
-        halo_arrived(odd, c)
+        halo_arrived(direct, c)
         halo_arrived(2, c)
         halo_arrived(3, c)
         return carry
 
     lax.fori_loop(0, per, arrived, 0)
+
+    def pass_on(c):
+        gather(0, c).wait_recv()
+        gather(2, c).start()
 
     def attend(c, carry):
         for j in range(K_NB):
@@ -170,10 +178,9 @@
         gather(0, c).start()
         gather(1, c).start()
 
-        @pl.when(c > 0)
+        @pl.when(c > 1)
         def _():
-            gather(0, c - 1).wait_recv()
-            gather(2, c - 1).start()
+            pass_on(c - 2)
 
         return carry
 
@@ -189,10 +196,9 @@
         second_sum(c).start()
 
     def mlp(c, carry):
-        @pl.when(c == 0)
+        @pl.when(c < 2)
         def _():
-            gather(0, per - 1).wait_recv()
-            gather(2, per - 1).start()
+            pass_on(per - 2 + c)
 
         gather(1, c).wait_recv()
         gather(2, c).wait_recv()
@@ -229,7 +235,9 @@
     lax.fori_loop(0, per, finish, 0)
 
     def sent(c, carry):
-        for kind in range(4):
+        for kind in range(2):
+            reach(kind, c).wait_send()
+        for kind in (2, 3):
             halo(kind, c).wait_send()
         for kind in range(3):
             gather(kind, c).wait_send()

time: 58.3 us -> 52.9 us (0.907)
  Pallas kernels: 56.5 us -> 51.1 us
    pallas_call x1, Pallas kernels: 56.5 us -> 51.1 us  [per_device(): pl.pallas_call(functools.partial(kernel, n, per), out_shape=jax.ShapeDtyp...]
where the time goes in v3:
time: 52.9 us; the launch traced here: 52.7 us
  Pallas kernels  51.1 us (97%)
  local copies, waits for them, and re-layouts  1.67 us (3%)
    pallas_call x1, Pallas kernels, per_device(): pl.pallas_call(functools.partial(kernel, n, per), out_shape=jax.ShapeDtyp...  51.1 us
    unnamed x1, local copies, waits for them, and re-layouts  1.67 us

profile of v3, /device:TPU:0, one launch (start us, length us, event | category | flops | bytes accessed | tf_op | source)
XLA Modules:
  0.0 52.7 jit_solution(12197804106032586668)
XLA Ops:
  0.0 51.1 %shard_map.82 = bf16[512,256]{1,0:T(8,128)(2,1)} custom-call(s32[8,32]{1,0:T(8,128)} %bitcast.3, bf16[512,1024]{1,0:T(8,128)(2,1)} %feats_in.1, f32[1,1024]{1,0:T(1,128)} %bitcast.4, bf16[3,1024,256]{2,1,0:T(8,128)(2,1)} %w_qkv_in.1, bf16[256,1024]{1,0:T(8,128)(2,1)} %w_out_in.1, f32[1,1024]{1,0:T(1,128)} %bitcast.5, bf16[1024,512]{1,0:T(8,128)(2,1)} %w_up_in.1, ...), custom_call_target="tpu_custom_call" | custom-call | tf_op jit(solution)/shard_map/pallas_call | solution.py:262
  51.1 1.7 %copy.10 = bf16[512,256]{1,0:T(8,128)(2,1)} copy(bf16[512,256]{1,0:T(8,128)(2,1)} %shard_map.82) | data formatting | bytes 524288
